TPU v7x, 128 devices: a whole 4x4x4 slice. The times are simulated.
128 devices in a mesh: dp: 16 (over y_lo, z, core), tensor: 8 (over x, y_hi).
Axes of the slice: x: 4, y: 4 (y_hi: 2, y_lo: 2; y = y_hi * 2 + y_lo), z: 4, core: 2. Of those that a mesh axis runs over, the one named last changes fastest.
Arguments:
- teacher_context: bfloat16 [20480, 8192], P('dp', 'tensor'), may hold values from -6 to 6
- teacher_out_weight: bfloat16 [8192, 4096], P('tensor'), may hold values from -0.0625 to 0.0625
- teacher_resid: bfloat16 [20480, 4096], P(('dp', 'tensor')), may hold values from -360 to 360
- teacher_gain: float32 [4096], replicated, may hold values from 0.1 to 1.9
- projector: bfloat16 [4096, 2048], P('tensor'), may hold values from -0.09375 to 0.09375
- student_context: bfloat16 [20480, 2048], P(('dp', 'tensor')), may hold values from -24 to 24
- student_resid: bfloat16 [20480, 2048], P(('dp', 'tensor')), may hold values from -6 to 6
- student_weight: bfloat16 [2048, 2048], P(('dp', 'tensor')), may hold values from -0.125 to 0.125
Outputs:
- weight_grad: float32 [2048, 2048], P(('dp', 'tensor'))
All inputs are finite; a program needn't handle non-finite values.
Results may differ from a plain program's by a relative error of at most 0.012.
Values may be sent and summed in bfloat16 or wider, within the bound.
A program may use at most 128 MiB of HBM per device.

v0:
```python
import jax
import jax.numpy as jnp
from jax import lax
from jax.sharding import PartitionSpec as P


def per_device(
    teacher_context,
    teacher_out_weight,
    teacher_resid,
    teacher_gain,
    projector,
    student_context,
    student_resid,
    student_weight,
):
    tensor_size = lax.axis_size("tensor")
    tok_rows = student_context.shape[0]
    total_tokens = tok_rows * lax.axis_size("dp") * tensor_size
    block_rows = teacher_context
    attended = lax.psum_scatter(
        jnp.dot(block_rows, teacher_out_weight, preferred_element_type=jnp.float32).astype(
            jnp.bfloat16
        ),
        "tensor",
        scatter_dimension=0,
        tiled=True,
    ).astype(jnp.float32)
    hidden = teacher_resid.astype(jnp.float32) + attended
    inverse = lax.rsqrt(jnp.mean(hidden * hidden, axis=-1, keepdims=True) + 1e-05)
    normed = (hidden * inverse * teacher_gain).astype(jnp.bfloat16)
    spread = lax.all_to_all(normed, "tensor", split_axis=1, concat_axis=0, tiled=True)
    block_rows = spread
    target = lax.psum_scatter(
        jnp.dot(block_rows, projector, preferred_element_type=jnp.float32).astype(jnp.bfloat16),
        "tensor",
        scatter_dimension=0,
        tiled=True,
    ).astype(jnp.float32)
    columns = student_context
    projected_out = jnp.dot(
        columns,
        lax.all_gather(student_weight, ("dp", "tensor"), axis=0, tiled=True),
        preferred_element_type=jnp.float32,
    )
    student_out = student_resid.astype(jnp.float32) + projected_out
    out_grad = (128.0 / total_tokens * (student_out - target)).astype(jnp.bfloat16)
    columns = student_context
    return lax.psum_scatter(
        lax.dot_general(
            columns, out_grad, (((0,), (0,)), ((), ())), preferred_element_type=jnp.float32
        ),
        ("dp", "tensor"),
        scatter_dimension=0,
        tiled=True,
    )


def solution(mesh):
    return jax.shard_map(
        per_device,
        mesh=mesh,
        in_specs=(
            P("dp", "tensor"),
            P("tensor", None),
            P(("dp", "tensor"), None),
            P(),
            P("tensor", None),
            P(("dp", "tensor"), None),
            P(("dp", "tensor"), None),
            P(("dp", "tensor"), None),
        ),
        out_specs=P(("dp", "tensor"), None),
        check_vma=False,
    )
```

profile of v0, /device:TPU:1, one launch (start us, length us, event | category | flops | bytes accessed | tf_op | source)
XLA Modules:
  0.0 1152.4 jit_solution(9007821223658147288)
XLA Ops:
  7.4 0.0 copy-start
  7.4 0.0 reduce-scatter.6.cloned.1.call-start
  7.4 1.7 copy-done
  9.1 16.5 %convolution_convert_fusion = bf16[1280,4096]{1,0:T(8,128)(2,1)} fusion(bf16[1280,1024]{1,0:T(8,128)(2,1)S(1)} %copy-done, bf16[1024,4096]{1,0:T(8,128)(2,1)} %param.9), kind=kOutput, calls=%fused_computation | convolution fusion | flops 10742661120 | bytes 21495808 | tf_op jit(solution)/shard_map/dot_general | solution.py:22
  25.6 0.0 copy-start.2
  25.6 0.0 reduce-scatter.6.cloned.1.call-update
  25.6 0.0 copy-start.6
  25.6 0.0 all-gather.2.cloned.1.call-start
  25.7 0.5 all-gather.2.cloned.1.call-update
  26.2 0.0 reduce-scatter.8.cloned.1.call-start
  26.3 137.7 %reduce-scatter.6.cloned.1.call-done = bf16[160,4096]{1,0:T(8,128)(2,1)} async-done(((bf16[1280,4096]{1,0:T(8,128)(2,1)}), bf16[160,4096]{1,0:T(8,128)(2,1)}) %reduce-scatter.6.cloned.1.call-update) | async-done | bytes 1310736 | tf_op jit(solution)/shard_map/reduce_scatter | solution.py:21
  163.9 0.0 copy-done.2
  163.9 1.9 multiply_reduce_fusion
  165.9 0.0 copy-done.6
  165.9 0.0 copy-done.3
  165.9 0.5 multiply_convert_fusion
  166.4 0.0 copy-start.7
  166.4 0.1 copy.18
  166.5 21.8 %all_to_all.19 = bf16[160,8,512]{2,0,1:T(8,128)(2,1)S(1)} all-to-all(bf16[160,8,512]{2,0,1:T(8,128)(2,1)S(1)} %bitcast.18), channel_id=1, replica_groups=mesh['dp'=16,'tensor'=8] {'tensor'}, dimensions={1} | all-to-all | bytes 2621440 | tf_op jit(solution)/shard_map/all_to_all | solution.py:32
  188.4 0.0 copy-done.7
  188.4 4.6 convolution_convert_fusion.1
  193.0 0.0 reduce-scatter.8.cloned.1.call-update
  193.0 0.0 reduce-scatter.10.cloned.1.call-start
  193.1 250.6 %all-gather.2.cloned.1.call-done = bf16[2048,2048]{1,0:T(8,128)(2,1)} async-done(((bf16[16,2048]{1,0:T(8,128)(2,1)}), bf16[2048,2048]{1,0:T(8,128)(2,1)}) %all-gather.2.cloned.1.call-update) | async-done | bytes 8388624 | tf_op jit(solution)/shard_map/all_gather | solution.py:43
  443.7 0.0 copy-done.4
  443.7 0.0 copy-done.5
  443.7 13.1 %convolution_bitcast_fusion = f32[2048,2048]{0,1:T(8,128)} fusion(bf16[160,2048]{1,0:T(8,128)(2,1)S(1)} %copy-done.4, bf16[2048,2048]{1,0:T(8,128)(2,1)} %all-gather.2.cloned.1.call-done, bf16[160,2048]{1,0:T(8,128)(2,1)} %reduce-scatter.8.cloned.1.call-done, bf16[160,2048]{1,0:T(8,128)(2,1)S(1)} %copy-done.5), kind=kOutput, calls=%fused_computation.1 | convolution fusion | flops 2686320640 | bytes 27131904 | tf_op jit(solution)/shard_map/dot_general | solution.py:50
  456.8 17.7 %copy.14 = f32[2048,2048]{1,0:T(8,128)} copy(f32[2048,2048]{0,1:T(8,128)} %convolution_bitcast_fusion) | data formatting | bytes 33554432
  474.5 0.0 reduce-scatter.10.cloned.1.call-update
  474.5 0.0 copy-start.1
  474.5 670.4 %reduce-scatter.10.cloned.1.call-done = f32[16,2048]{1,0:T(8,128)} async-done(((f32[2048,2048]{1,0:T(8,128)}), f32[16,2048]{1,0:T(8,128)}) %reduce-scatter.10.cloned.1.call-update) | async-done | bytes 131088 | tf_op jit(solution)/shard_map/reduce_scatter | solution.py:49
  1145.0 0.0 copy-done.1
  (5 shorter events, 0.0 us)
Async XLA Ops:
  7.4 1.7 copy-start
  7.4 156.5 %reduce-scatter.6.cloned.1.call-start = ((), (), s32[]{:S(2)}) async-start(), calls=%async_computation.5 | async-start | bytes 11796480 | tf_op jit(solution)/shard_map/reduce_scatter | solution.py:21
  25.6 138.3 %copy-start.2 = (bf16[160,4096]{1,0:T(8,128)(2,1)S(1)}, bf16[160,4096]{1,0:T(8,128)(2,1)}, u32[]{:S(2)}) copy-start(bf16[160,4096]{1,0:T(8,128)(2,1)} %param.10) | copy-start | bytes 3932164
  25.6 140.3 %copy-start.6 = (f32[4096]{0:T(1024)S(1)}, f32[4096]{0:T(1024)}, u32[]{:S(2)}) copy-start(f32[4096]{0:T(1024)} %param.11) | copy-start | bytes 49156
  25.6 418.1 %all-gather.2.cloned.1.call-start = ((), (), s32[]{:S(2)}) async-start(), calls=%async_computation.4 | async-start | bytes 8454144 | tf_op jit(solution)/shard_map/all_gather | solution.py:43
  26.2 417.5 %reduce-scatter.8.cloned.1.call-start = ((), (), s32[]{:S(2)}) async-start(), calls=%async_computation.6 | async-start | bytes 5898240 | tf_op jit(solution)/shard_map/reduce_scatter | solution.py:34
  163.9 1.9 copy-start.3
  166.4 22.0 %copy-start.7 = (bf16[512,2048]{1,0:T(8,128)(2,1)S(1)}, bf16[512,2048]{1,0:T(8,128)(2,1)}, u32[]{:S(2)}) copy-start(bf16[512,2048]{1,0:T(8,128)(2,1)} %param.12) | copy-start | bytes 6291460
  193.0 250.7 %copy-start.4 = (bf16[160,2048]{1,0:T(8,128)(2,1)S(1)}, bf16[160,2048]{1,0:T(8,128)(2,1)}, u32[]{:S(2)}) copy-start(bf16[160,2048]{1,0:T(8,128)(2,1)} %param.13) | copy-start | bytes 1966084
  193.0 250.7 %copy-start.5 = (bf16[160,2048]{1,0:T(8,128)(2,1)S(1)}, bf16[160,2048]{1,0:T(8,128)(2,1)}, u32[]{:S(2)}) copy-start(bf16[160,2048]{1,0:T(8,128)(2,1)} %param.14) | copy-start | bytes 1966084
  193.0 951.9 %reduce-scatter.10.cloned.1.call-start = ((), (), s32[]{:S(2)}) async-start(), calls=%async_computation.7 | async-start | bytes 16908288 | tf_op jit(solution)/shard_map/reduce_scatter | solution.py:49
  474.5 670.4 %copy-start.1 = (bf16[1280,1024]{1,0:T(8,128)(2,1)S(1)}, bf16[1280,1024]{1,0:T(8,128)(2,1)}, u32[]{:S(2)}) copy-start(bf16[1280,1024]{1,0:T(8,128)(2,1)} %param.8) | copy-start | bytes 7864324
Sparse Core Ops, SparseCore 0:
  25.7 138.1 reduce-scatter.5
  193.2 94.0 reduce-scatter.7
Sparse Core Ops, SparseCore 1:
  27.8 415.9 all-gather.1
  474.6 670.3 reduce-scatter.9
where the time goes:
time: 1160 us; the launch traced here: 1150 us
  waiting for transfers between devices  1060 us (91%)
  matrix products  34.2 us (3%)
  blocking collectives  21.8 us (2%)
  local copies, waits for them, and re-layouts  19.5 us (2%)
  between operations  14.9 us (1%)
    reduce_scatter x1, waiting for transfers between devices, per_device(): lax.psum_scatter(lax.dot_general(columns, out_grad, (((0,), (0,)), ((), (...  670 us
    all_gather x1, waiting for transfers between devices, per_device(): lax.all_gather(student_weight, ('dp', 'tensor'), axis=0, tiled=True)  251 us
    reduce_scatter x1, waiting for transfers between devices, per_device(): lax.psum_scatter(jnp.dot(block_rows, teacher_out_weight, preferred_elemen...  138 us
  transfers between devices with their start and end apart: 4, of which 3 were waited for; matrix products, arithmetic and copies ran while one was open for 1% of the time, Pallas kernels for 0%

commit v1 on v0

v1 whole, which is shorter than its diff:
```python
import jax
import jax.numpy as jnp
from jax import lax
from jax.experimental import pallas as pl
from jax.experimental.pallas import tpu as pltpu
from jax.sharding import PartitionSpec as P

MESH = pl.DeviceIdType.MESH
BF16 = jnp.bfloat16
F32 = jnp.float32

GATHER_PARTS = ((0, 768, "y"), (768, 256, "z"))
GRAD_PARTS = ((0, 384, "xyz"), (384, 384, "yzx"), (768, 256, "zxy"))
N_SEM = 176
N_LOCAL = 20
CHUNKS = 4


def step(v, by):
    return lax.rem(v + by, 4)


class Net:
    def __init__(self, send_sems, recv_sems, local_sems):
        dp, t = lax.axis_index("dp"), lax.axis_index("tensor")
        self.x = lax.div(t, 2)
        self.y = lax.rem(t, 2) * 2 + lax.div(dp, 8)
        self.z = lax.rem(lax.div(dp, 2), 4)
        self.c = lax.rem(dp, 2)
        self.send_sems, self.recv_sems, self.local_sems = send_sems, recv_sems, local_sems
        self.used = self.used_local = 0
        self.sent = []

    def at(self, x=0, y=0, z=0, c=0):
        px, py, pz = step(self.x, x), step(self.y, y), step(self.z, z)
        pc = lax.rem(self.c + c, 2)
        return (lax.rem(py, 2) * 8 + pz * 2 + pc, px * 2 + lax.div(py, 2))

    def send(self, src, dst, **where):
        i = self.used
        self.used += 1
        copy = pltpu.make_async_remote_copy(
            src_ref=src,
            dst_ref=dst,
            send_sem=self.send_sems.at[i],
            recv_sem=self.recv_sems.at[i],
            device_id=self.at(**where),
            device_id_type=MESH,
        )
        copy.start()
        self.sent.append(copy)
        return copy

    def load(self, src, dst):
        i = self.used_local
        self.used_local += 1
        copy = pltpu.make_async_copy(src, dst, self.local_sems.at[i])
        copy.start()
        return copy


def kernel(
    a_in, w_in, r_in, gain, p_in, s_in, sr_in, ws_in, out,
    a_v, w_v, c_v, ra, rb, ry, h_v, r_v, n_v, p_v, ws_v, s_v, sr_v, so_v, g_v, grad, o_recv, o_send,
    rg00, rg01, rg02, rg10, rg11, rg12, rg20, rg21, rg22,
    send_sems, recv_sems, local_sems,
):
    rg = ((rg00, rg01, rg02), (rg10, rg11, rg12), (rg20, rg21, rg22))
    net = Net(send_sems, recv_sems, local_sems)
    x, y, z, c = net.x, net.y, net.z, net.c
    other_c = 1 - c
    yh, yl = lax.div(y, 2), lax.rem(y, 2)
    other_yh = 1 - yh
    mine = pl.ds(pl.multiple_of(c * 1024, 1024), 1024)
    theirs = pl.ds(pl.multiple_of(other_c * 1024, 1024), 1024)

    load_a = net.load(a_in, a_v)
    w_loads = {}

    def load_w(n):
        k = n % CHUNKS
        w_loads[n] = net.load(w_in.at[:, pl.ds(k * 1024, 1024)], w_v.at[n % 2])

    load_w(0)
    load_w(1)
    early = [
        net.load(p_in.at[yl, z, :, mine], p_v.at[x, yh, yl, z]),
        net.load(ws_in.at[:, mine], ws_v.at[yl, z, c, x, yh]),
        net.load(s_in, s_v.at[c]),
        net.load(sr_in.at[:, mine], sr_v.at[c]),
        net.load(r_in, r_v),
    ]

    partners = [dict(c=1)] + [{axis: by} for axis in "xyz" for by in (1, 2, 3)]
    barrier = pltpu.get_barrier_semaphore()
    for where in partners:
        pl.semaphore_signal(barrier, inc=1, device_id=net.at(**where), device_id_type=MESH)
    pl.semaphore_wait(barrier, len(partners))

    ws_pair = net.send(ws_in.at[:, theirs], ws_v.at[yl, z, c, x, yh], c=1)
    p_x = [net.send(p_in.at[yl, z, :, mine], p_v.at[x, yh, yl, z], x=by) for by in (1, 3, 2)]
    s_pair = net.send(s_in, s_v.at[c], c=1)
    sr_pair = net.send(sr_in.at[:, theirs], sr_v.at[c], c=1)

    def product(rel, k, slot):
        rows = step(x, rel)

        @pl.loop(0, 4)
        def _(j):
            cols = pl.ds(pl.multiple_of(j * 256, 256), 256)
            res = jnp.dot(a_v[rows], w_v[slot, :, cols], preferred_element_type=F32).astype(BF16)
            c_v[rel, k, 0, :, cols] = res[:160]
            c_v[rel, k, 1, :, cols] = res[160:]

    far = {}
    direct = {}
    relayed = {}
    ysent = {}

    def far_products():
        load_a.wait()
        for k in range(CHUNKS):
            w_loads[k].wait()
            product(2, k, k % 2)
            far[k] = (
                net.send(c_v.at[2, k, 0], ra.at[0, k], x=1),
                net.send(c_v.at[2, k, 1], ra.at[1, k], x=3),
            )
            load_w(k + 2)

    def near_products(k):
        n = CHUNKS + k
        w_loads[n].wait()
        product(1, k, n % 2)
        one = net.send(c_v.at[1, k, 1], rb.at[0, 1, k], x=1)
        product(3, k, n % 2)
        direct[k] = (one, net.send(c_v.at[3, k, 0], rb.at[1, 0, k], x=3))

    def relay(k):
        far[k][0].wait_recv()
        c_v[1, k, 0] = (c_v[1, k, 0].astype(F32) + ra[0, k].astype(F32)).astype(BF16)
        one = net.send(c_v.at[1, k, 0], rb.at[0, 0, k], x=1)
        far[k][1].wait_recv()
        c_v[3, k, 1] = (c_v[3, k, 1].astype(F32) + ra[1, k].astype(F32)).astype(BF16)
        relayed[k] = (one, net.send(c_v.at[3, k, 1], rb.at[1, 1, k], x=3))
        n = CHUNKS + k
        product(0, k, n % 2)
        if n + 2 < 2 * CHUNKS:
            load_w(n + 2)

    def x_sum(k):
        for copy in direct[k] + relayed[k]:
            copy.wait_recv()

        def total(h):
            return c_v[0, k, h].astype(F32) + rb[0, h, k].astype(F32) + rb[1, h, k].astype(F32)

        c_v[0, k, other_yh] = total(other_yh).astype(BF16)
        ysent[k] = net.send(c_v.at[0, k, other_yh], ry.at[k], y=2)
        cols = pl.ds(k * 1024, 1024)
        h_v[:, cols] = total(yh) + r_v[:, cols].astype(F32)

    squares = []

    def y_sum(k):
        ysent[k].wait_recv()
        cols = pl.ds(k * 1024, 1024)
        hidden = h_v[:, cols] + ry[k].astype(F32)
        h_v[:, cols] = hidden
        squares.append(jnp.sum(hidden * hidden, axis=-1, keepdims=True))

    def piece(yv, zv, start, width):
        h, l, cols = lax.div(yv, 2), lax.rem(yv, 2), pl.ds(start, width)
        return p_v.at[:, h, l, zv, :, cols], ws_v.at[l, zv, :, :, h, :, cols]

    gathers = {}

    def gather_send(key, yv, zv, start, width, axis, by):
        gathers[key] = [net.send(ref, ref, **{axis: by}) for ref in piece(yv, zv, start, width)]

    def gather_wait(*key):
        for copy in gathers[key]:
            copy.wait_recv()

    place = {"y": y, "z": z}

    def ring(part, axis, item):
        start, width, _ = GATHER_PARTS[part]
        yz = (y, step(z, item)) if axis == "y" else (step(y, item), z)
        for by in (1, 3):
            gather_send((part, axis, item, by), *yz, start, width, axis, by)

    def onward(part, axis, item):
        start, width, _ = GATHER_PARTS[part]
        half = width // 2
        for by, begin in ((1, start), (3, start + half)):
            gather_wait(part, axis, item, by)
            source = step(place[axis], 4 - by)
            yz = (source, step(z, item)) if axis == "y" else (step(y, item), source)
            gather_send((part, axis, item, by, "on"), *yz, begin, half, axis, by)

    def arrived(part, axis, item):
        for by in (1, 3):
            gather_wait(part, axis, item, by, "on")

    def gather_x():
        for copy in early[:2]:
            copy.wait()
        ws_pair.wait_recv()
        ref = ws_v.at[yl, z, :, x, yh]
        return [net.send(ref, ref, x=by) for by in (1, 3, 2)]

    def gather_begin(ws_x):
        for copy in p_x + ws_x:
            copy.wait_recv()
        ring(1, "z", 0)
        ring(0, "y", 0)
        ring(0, "z", 0)
        ring(1, "y", 0)

    ws_x = gather_x()
    far_products()
    gather_begin(ws_x)
    near_products(0)
    relay(0)
    onward(1, "z", 0)
    near_products(1)
    relay(1)
    onward(0, "y", 0)
    ring(0, "z", 3)
    ring(0, "z", 1)
    onward(0, "z", 0)
    ring(1, "y", 3)
    ring(1, "y", 1)
    near_products(2)
    relay(2)
    arrived(1, "z", 0)
    ring(1, "y", 2)
    onward(1, "y", 0)
    arrived(0, "y", 0)
    ring(0, "z", 2)
    near_products(3)
    relay(3)
    for copy in early[2:]:
        copy.wait()
    onward(1, "y", 3)
    onward(1, "y", 1)
    onward(0, "z", 3)
    x_sum(0)
    onward(1, "y", 2)
    onward(0, "z", 1)
    y_sum(0)
    x_sum(1)
    y_sum(1)
    onward(0, "z", 2)
    x_sum(2)
    y_sum(2)
    s_pair.wait_recv()
    sr_pair.wait_recv()
    for item in range(4):
        arrived(0, "z", item)
        arrived(1, "y", item)

    @pl.loop(0, 4)
    def _(j):
        cols = pl.ds(pl.multiple_of(j * 256, 256), 256)
        so_v[:, cols] = sr_v[:, :, cols].reshape(320, 256).astype(F32) + jnp.dot(
            s_v[...].reshape(320, 2048),
            ws_v[:, :, :, :, :, :, cols].reshape(2048, 256),
            preferred_element_type=F32,
        )

    x_sum(3)
    y_sum(3)

    inverse = lax.rsqrt(sum(squares) * (1.0 / 4096.0) + 1e-05)
    n_pair = []
    for k in range(CHUNKS):
        cols = pl.ds(k * 1024, 1024)
        n_v[c, :, cols] = (h_v[:, cols] * inverse * gain[:, cols]).astype(BF16)
        n_pair.append(net.send(n_v.at[c, :, cols], n_v.at[c, :, cols], c=1))
    for k in range(CHUNKS):
        n_pair[k].wait_recv()

        @pl.loop(0, 4)
        def _(j):
            cols = pl.ds(pl.multiple_of(j * 256, 256), 256)
            so_v[:, cols] -= jnp.dot(
                n_v[:, :, pl.ds(k * 1024, 1024)].reshape(320, 1024),
                p_v[k, :, :, :, :, cols].reshape(1024, 256),
                preferred_element_type=F32,
            )

    g_v[...] = (128.0 / 20480.0 * so_v[...]).astype(BF16)

    def grad_piece(yv, zv, xv, cols):
        every = slice(None)
        l, h = (every, every) if yv is None else (lax.rem(yv, 2), lax.div(yv, 2))
        return (l, every if zv is None else zv, every, every if xv is None else xv, h, every, cols)

    where = {"x": x, "y": y, "z": z}
    fixed = [dict(x=None, y=None, z=None) for _ in GRAD_PARTS]
    grads = {}

    def grad_send(part, stage):
        start, width, order = GRAD_PARTS[part]
        axis = order[stage]
        cols = pl.ds(start, width)
        for rel in (1, 3, 2):
            to = dict(fixed[part])
            to[axis] = step(where[axis], rel)
            ref = grad.at[grad_piece(to["y"], to["z"], to["x"], cols)]
            grads[part, stage, rel] = net.send(ref, rg[part][stage].at[rel - 1], **{axis: rel})
        fixed[part][axis] = where[axis]

    def grad_sum(part, stage):
        start, width, order = GRAD_PARTS[part]
        for rel in (1, 3, 2):
            grads[part, stage, rel].wait_recv()
        own = grad_piece(fixed[part]["y"], fixed[part]["z"], fixed[part]["x"], pl.ds(start, width))
        total = grad[own].astype(F32)
        for i in range(3):
            total = total + rg[part][stage][i].astype(F32)
        return own, total

    for part, (start, width, order) in enumerate(GRAD_PARTS):
        cols = pl.ds(start, width)

        @pl.loop(0, 8)
        def _(i):
            rows = pl.ds(pl.multiple_of(i * 256, 256), 256)
            res = lax.dot_general(
                s_v[:, :, rows].reshape(320, 256),
                g_v[:, cols],
                (((0,), (0,)), ((), ())),
                preferred_element_type=F32,
            )
            grad[lax.div(i, 4), lax.rem(i, 4), :, :, :, :, cols] = res.astype(BF16).reshape(2, 4, 2, 16, width)

        grad_send(part, 0)

    for stage in range(2):
        for part in range(3):
            own, total = grad_sum(part, stage)
            grad[own] = total.astype(BF16)
            grad_send(part, stage + 1)

    last = []
    for part, (start, width, _) in enumerate(GRAD_PARTS):
        _, total = grad_sum(part, 2)
        cols = pl.ds(start, width)
        o_send[:, :, cols] = total
        ref = o_send.at[other_c, :, cols]
        last.append(net.send(ref, o_recv.at[:, cols], c=1))
    for copy in last:
        copy.wait_recv()
    out[:, mine] = o_send[c]
    out[:, theirs] = o_recv[...]

    for copy in net.sent:
        copy.wait_send()


def grad_scratch():
    shapes = []
    for _, width, order in GRAD_PARTS:
        done = set()
        for axis in order:
            done.add(axis)
            dims = [] if "y" in done else [2]
            dims += [] if "z" in done else [4]
            dims += [2]
            dims += [] if "x" in done else [4]
            dims += [] if "y" in done else [2]
            shapes.append(pltpu.VMEM((3, *dims, 16, width), BF16))
    return shapes


def per_device(a, w, resid, gain, projector, s, s_resid, ws):
    anywhere = pl.BlockSpec(memory_space=pl.ANY)
    vmem = pl.BlockSpec(memory_space=pltpu.VMEM)
    return pl.pallas_call(
        kernel,
        out_shape=jax.ShapeDtypeStruct((16, 2048), F32),
        in_specs=[anywhere, anywhere, anywhere, vmem, anywhere, anywhere, anywhere, anywhere],
        out_specs=vmem,
        scratch_shapes=[
            pltpu.VMEM((4, 320, 1024), BF16),
            pltpu.VMEM((2, 1024, 1024), BF16),
            pltpu.VMEM((4, CHUNKS, 2, 160, 1024), BF16),
            pltpu.VMEM((2, CHUNKS, 160, 1024), BF16),
            pltpu.VMEM((2, 2, CHUNKS, 160, 1024), BF16),
            pltpu.VMEM((CHUNKS, 160, 1024), BF16),
            pltpu.VMEM((160, 4096), F32),
            pltpu.VMEM((160, 4096), BF16),
            pltpu.VMEM((2, 160, 4096), BF16),
            pltpu.VMEM((4, 2, 2, 4, 64, 1024), BF16),
            pltpu.VMEM((2, 4, 2, 4, 2, 16, 1024), BF16),
            pltpu.VMEM((2, 160, 2048), BF16),
            pltpu.VMEM((2, 160, 1024), BF16),
            pltpu.VMEM((320, 1024), F32),
            pltpu.VMEM((320, 1024), BF16),
            pltpu.VMEM((2, 4, 2, 4, 2, 16, 1024), BF16),
            pltpu.VMEM((16, 1024), F32),
            pltpu.VMEM((2, 16, 1024), F32),
            *grad_scratch(),
            pltpu.SemaphoreType.DMA((N_SEM,)),
            pltpu.SemaphoreType.DMA((N_SEM,)),
            pltpu.SemaphoreType.DMA((N_LOCAL,)),
        ],
        compiler_params=pltpu.CompilerParams(
            collective_id=0, has_side_effects=True, vmem_limit_bytes=62 * 2**20
        ),
        cost_estimate=pl.CostEstimate(flops=16 * 10**9, bytes_accessed=16 * 10**6, transcendentals=160),
    )(
        a.reshape(4, 320, 1024),
        w,
        resid,
        gain.reshape(1, 4096),
        projector.reshape(2, 4, 64, 2048),
        s,
        s_resid,
        ws,
    )


def solution(mesh):
    return jax.shard_map(
        per_device,
        mesh=mesh,
        in_specs=(
            P("dp", "tensor"),
            P("tensor", None),
            P(("dp", "tensor"), None),
            P(),
            P("tensor", None),
            P(("dp", "tensor"), None),
            P(("dp", "tensor"), None),
            P(("dp", "tensor"), None),
        ),
        out_specs=P(("dp", "tensor"), None),
        check_vma=False,
    )
```

time: 1160 us -> 161 us (0.14)
  waiting for transfers between devices: 1060 us -> 0 us
  Pallas kernels: 0 us -> 159 us
  matrix products: 34.2 us -> 0 us
  blocking collectives: 21.8 us -> 0 us
  local copies, waits for them, and re-layouts: 19.5 us -> 1.57 us
  between operations: 14.9 us -> 0.01 us
    reduce_scatter x3 -> x0, waiting for transfers between devices: 808 us -> none  [the longest x1 670 us: per_device(): lax.psum_scatter(lax.dot_general(columns, out_grad, (((0,), (0,)), ((), (...]
    all_gather x1 -> x0, waiting for transfers between devices: 251 us -> none  [per_device(): lax.all_gather(student_weight, ('dp', 'tensor'), axis=0, tiled=True)]
    pallas_call x0 -> x1, Pallas kernels: none -> 159 us  [per_device(): pl.pallas_call(kernel, out_shape=jax.ShapeDtypeStruct((16, 2048), F32), i...]
    dot_general x3 -> x0, matrix products: 34.2 us -> none  [the longest x1 16.5 us: per_device(): jnp.dot(block_rows, teacher_out_weight, preferred_element_type=jnp.float32)]
    all_to_all x1 -> x0, blocking collectives: 21.8 us -> none  [per_device(): lax.all_to_all(normed, 'tensor', split_axis=1, concat_axis=0, tiled=True)]
    unnamed x17 -> x1, local copies, waits for them, and re-layouts: 19.4 us -> 1.57 us
  transfers between devices with their start and end apart: 4 -> 0, of which waited for: 3 -> 0; matrix products, arithmetic and copies ran while one was open for 1% -> 0% of each run, Pallas kernels for 0% -> 0%
where the time goes in v1:
time: 161 us
  Pallas kernels  159 us (99%)
    pallas_call x1, Pallas kernels, per_device(): pl.pallas_call(kernel, out_shape=jax.ShapeDtypeStruct((16, 2048), F32), i...  159 us

profile of v1, /device:TPU:1, one launch (start us, length us, event | category | flops | bytes accessed | tf_op | source)
XLA Modules:
  0.0 161.0 jit_solution(188351655406964674)
XLA Ops:
  0.0 159.4 %shard_map.82 = f32[16,2048]{1,0:T(8,128)} custom-call(bf16[4,320,1024]{2,1,0:T(8,128)(2,1)} %bitcast.3, bf16[1024,4096]{1,0:T(8,128)(2,1)} %w_in.1, bf16[160,4096]{1,0:T(8,128)(2,1)} %r_in.1, f32[1,4096]{1,0:T(1,128)} %bitcast.5, bf16[2,4,64,2048]{3,2,1,0:T(8,128)(2,1)} %bitcast.4, bf16[160,2048]{1,0:T(8,128)(2,1)} %s_in.1, bf16[160,2048]{1,0:T(8,128)(2,1)} %sr_in.1, ...), custom_call_target="tpu_custom_call" | custom-call | flops 16000000000 | bytes 16000000 | tf_op jit(solution)/shard_map/pallas_call | solution.py:382
  159.4 1.6 copy.10

commit v2 on v0

v2 whole, which is shorter than its diff:
```python
import jax
import jax.numpy as jnp
from jax import lax
from jax.experimental import pallas as pl
from jax.experimental.pallas import tpu as pltpu
from jax.sharding import PartitionSpec as P

MESH = pl.DeviceIdType.MESH
BF16 = jnp.bfloat16
F32 = jnp.float32

WIDE = 512
Y_FIRST = (3, 7)
W_ORDER = (2, 3, 6, 7, 1, 0, 4, 5)
N_SEM = 179
N_LOCAL = 16


def step(v, by):
    return lax.rem(v + by, 4)


class Net:
    def __init__(self, send_sems, recv_sems, local_sems):
        dp, t = lax.axis_index("dp"), lax.axis_index("tensor")
        self.x = lax.div(t, 2)
        self.y = lax.rem(t, 2) * 2 + lax.div(dp, 8)
        self.z = lax.rem(lax.div(dp, 2), 4)
        self.c = lax.rem(dp, 2)
        self.send_sems, self.recv_sems, self.local_sems = send_sems, recv_sems, local_sems
        self.used = self.used_local = 0
        self.sent = []

    def at(self, x=0, y=0, z=0, c=0):
        px, py, pz = step(self.x, x), step(self.y, y), step(self.z, z)
        pc = lax.rem(self.c + c, 2)
        return (lax.rem(py, 2) * 8 + pz * 2 + pc, px * 2 + lax.div(py, 2))

    def send(self, src, dst, **where):
        i = self.used
        self.used += 1
        copy = pltpu.make_async_remote_copy(
            src_ref=src,
            dst_ref=dst,
            send_sem=self.send_sems.at[i],
            recv_sem=self.recv_sems.at[i],
            device_id=self.at(**where),
            device_id_type=MESH,
        )
        copy.start()
        self.sent.append(copy)
        return copy

    def load(self, src, dst):
        i = self.used_local
        self.used_local += 1
        copy = pltpu.make_async_copy(src, dst, self.local_sems.at[i])
        copy.start()
        return copy


def kernel(
    a_in, w_in, r_in, gain, p_in, s_in, sr_in, ws_in, out,
    a_v, w_v, c_v, ra, rb, ry, ry4, r_v, hg_v, p_v, ws_t, ws_v, s_v, st_v, sr_t, sr_v, t_v, so_v, g_v,
    iv_v, grad, ga1, gb1, ga2, gb2, ra2, rb2, fin, o_r,
    send_sems, recv_sems, local_sems,
):
    net = Net(send_sems, recv_sems, local_sems)
    x, y, z, c = net.x, net.y, net.z, net.c
    other_c = 1 - c
    yh, yl = lax.div(y, 2), lax.rem(y, 2)
    other_yh = 1 - yh
    my_cols = pl.ds(pl.multiple_of(z * 512 + c * 256, 256), 256)
    mine = pl.ds(pl.multiple_of(c * 256, 256), 256)
    theirs = pl.ds(pl.multiple_of(other_c * 256, 256), 256)

    def slab(zv):
        return pl.ds(pl.multiple_of(zv * 512, 512), 512)

    load_a = net.load(a_in, a_v)
    w_loads = {}

    def load_w(n):
        if n < len(W_ORDER):
            w_loads[n] = net.load(w_in.at[:, pl.ds(W_ORDER[n] * WIDE, WIDE)], w_v.at[n % 2])

    load_w(0)
    load_w(1)
    load_p = net.load(p_in.at[yl, :, my_cols], p_v.at[x, yh, yl])
    load_ws = net.load(ws_in.at[:, slab(z)], ws_t.at[z])
    load_sr = net.load(sr_in.at[:, slab(z)], sr_t.at[z])
    load_s = net.load(s_in, s_v.at[z, c])
    load_r = net.load(r_in, r_v)

    partners = [dict(c=1)] + [{axis: by} for axis in "xyz" for by in (1, 2, 3)] + [dict(z=by, c=1) for by in (1, 2, 3)]
    barrier = pltpu.get_barrier_semaphore()
    for where in partners:
        pl.semaphore_signal(barrier, inc=1, device_id=net.at(**where), device_id_type=MESH)

    def ahead(by):
        return step(x, by)

    def products(k):
        n = W_ORDER.index(k)
        w_loads[n].wait()

        @pl.loop(0, WIDE // 256)
        def _(j):
            cols = pl.ds(pl.multiple_of(j * 256, 256), 256)
            res = jnp.dot(a_v[...].reshape(1280, 1024), w_v[n % 2, :, cols], preferred_element_type=F32)
            c_v[k, :, :, :, cols] = res.astype(BF16).reshape(4, 2, 160, 256)

        load_w(n + 2)

    far, direct, relayed, ysent = {}, {}, {}, {}

    def x_far(k):
        far[k] = (
            net.send(c_v.at[k, ahead(2), 0], ra.at[k, 0], x=1),
            net.send(c_v.at[k, ahead(2), 1], ra.at[k, 1], x=3),
        )

    def y_first_send(k, rel):
        ysent[k, rel] = net.send(c_v.at[k, ahead(rel), other_yh], ry4.at[Y_FIRST.index(k), rel], y=2)

    def x_direct(k):
        direct[k] = (
            net.send(c_v.at[k, ahead(1), 1], rb.at[k, 0, 1], x=1),
            net.send(c_v.at[k, ahead(3), 0], rb.at[k, 1, 0], x=3),
        )

    def x_relay(k):
        sends = []
        for way, rel, by in ((0, 1, 1), (1, 3, 3)):
            far[k][way].wait_recv()
            to = ahead(rel)
            c_v[k, to, way] = (c_v[k, to, way].astype(F32) + ra[k, way].astype(F32)).astype(BF16)
            sends.append(net.send(c_v.at[k, to, way], rb.at[k, way, way], x=by))
        relayed[k] = sends

    def x_total(k, h):
        return c_v[k, x, h].astype(F32) + rb[k, 0, h].astype(F32) + rb[k, 1, h].astype(F32)

    def x_sum(k):
        for copy in (*direct[k], *relayed[k]):
            copy.wait_recv()
        c_v[k, x, other_yh] = x_total(k, other_yh).astype(BF16)
        ysent[k] = net.send(c_v.at[k, x, other_yh], ry.at[k], y=2)

    squares = []
    hg = {}

    def hidden_out(k, hidden):
        cols = pl.ds(k * WIDE, WIDE)
        squares.append(jnp.sum(hidden * hidden, axis=-1, keepdims=True))
        hg_v[k, z, c] = (hidden * gain[:, cols]).astype(BF16)
        ref = hg_v.at[k, z, c]
        hg[k] = {by: net.send(ref, ref, z=by) for by in (1, 3)}
        hg[k]["pair"] = [net.send(ref, ref, c=1)]

    def y_sum(k):
        ysent[k].wait_recv()
        cols = pl.ds(k * WIDE, WIDE)
        hidden_out(k, r_v[:, cols].astype(F32) + x_total(k, yh) + ry[k].astype(F32))

    low, high = pl.ds(0, 80), pl.ds(80, 80)

    def y_first_add(k, rel):
        ysent[k, rel].wait_recv()
        to = ahead(rel)
        c_v[k, to, yh] = (c_v[k, to, yh].astype(F32) + ry4[Y_FIRST.index(k), rel].astype(F32)).astype(BF16)
        return to

    def y_first_far(k):
        to = y_first_add(k, 2)
        far[k] = (
            net.send(c_v.at[k, to, yh, low], ra.at[k, 0, low], x=1),
            net.send(c_v.at[k, to, yh, high], ra.at[k, 1, high], x=3),
        )

    def y_first_direct(k):
        one = net.send(c_v.at[k, y_first_add(k, 1), yh, high], rb.at[k, 0, 0, high], x=1)
        direct[k] = (one, net.send(c_v.at[k, y_first_add(k, 3), yh, low], rb.at[k, 1, 0, low], x=3))

    def y_first_relay(k):
        sends = []
        for way, rel, by, rows in ((0, 1, 1, low), (1, 3, 3, high)):
            far[k][way].wait_recv()
            to = ahead(rel)
            c_v[k, to, yh, rows] = (c_v[k, to, yh, rows].astype(F32) + ra[k, way, rows].astype(F32)).astype(BF16)
            sends.append(net.send(c_v.at[k, to, yh, rows], rb.at[k, way, 0, rows], x=by))
        relayed[k] = sends

    def y_first_out(k):
        for copy in (*direct[k], *relayed[k]):
            copy.wait_recv()
        cols = pl.ds(k * WIDE, WIDE)
        ysent[k, 0].wait_recv()
        total = c_v[k, x, yh].astype(F32) + ry4[Y_FIRST.index(k), 0].astype(F32)
        total = total + rb[k, 0, 0].astype(F32) + rb[k, 1, 0].astype(F32)
        hidden_out(k, r_v[:, cols].astype(F32) + total)

    def hg_on(k):
        hg[k]["on"] = []
        for by, rows in ((1, low), (3, high)):
            source = step(z, 4 - by)
            hg[k][by].wait_recv()
            ref = hg_v.at[k, source, c, rows]
            hg[k]["on"].append(net.send(ref, ref, z=by))
            ref = hg_v.at[k, source, c]
            hg[k]["pair"].append(net.send(ref, ref, c=1))

    def hg_end(k):
        for copy in hg[k]["on"]:
            copy.wait_recv()
        ref = hg_v.at[k, step(z, 2), c]
        hg[k]["pair"].append(net.send(ref, ref, c=1))

    def hg_dot(k):
        for copy in hg[k]["pair"]:
            copy.wait_recv()

        t_v[...] += jnp.dot(
            hg_v[k].reshape(1280, WIDE), p_v[k // 2, k % 2].reshape(WIDE, 256), preferred_element_type=F32
        ).reshape(4, 320, 256)

    def plane_x():
        load_p.wait()
        ref = p_v.at[x, yh, yl]
        return [net.send(ref, ref, x=by) for by in (1, 3, 2)]

    def ws_pair():
        load_ws.wait()
        for copy in ws_z:
            copy.wait_recv()
        copy = net.load(ws_t.at[:, :, mine], ws_v.at[yl, :, c, x, yh])
        return copy, net.send(ws_t.at[:, :, theirs], ws_v.at[yl, :, c, x, yh], c=1)

    def ws_x(pair):
        pair[0].wait()
        pair[1].wait_recv()
        ref = ws_v.at[yl, :, :, x, yh]
        return [net.send(ref, ref, x=by) for by in (1, 3, 2)]

    def p_at(yv, cols):
        return p_v.at[:, lax.div(yv, 2), lax.rem(yv, 2), :, cols]

    def ws_at(yv, cols):
        return ws_v.at[lax.rem(yv, 2), :, :, :, lax.div(yv, 2), :, cols]

    def plane_y(arriving, ref_at):
        for copy in arriving:
            copy.wait_recv()
        ref = ref_at(y, pl.ds(0, 256))
        return {by: net.send(ref, ref, y=by) for by in (1, 3)}

    def plane_y_on(ring, ref_at):
        sends = []
        for by, begin in ((1, 0), (3, 128)):
            ring[by].wait_recv()
            ref = ref_at(step(y, 4 - by), pl.ds(begin, 128))
            sends.append(net.send(ref, ref, y=by))
        return sends

    def s_on():
        sends = []
        for by, rows in ((1, low), (3, high)):
            source = step(z, 4 - by)
            s_ring[by].wait_recv()
            ref = s_v.at[source, c, rows]
            sends.append(net.send(ref, ref, z=by))
            ref = s_v.at[source, c]
            s_pair.append(net.send(ref, ref, c=1))
        return sends

    def s_end(sends):
        for copy in sends:
            copy.wait_recv()
        ref = s_v.at[step(z, 2), c]
        s_pair.append(net.send(ref, ref, c=1))

    def sr_end():
        load_sr.wait()
        for copy in sr_z:
            copy.wait_recv()
        return net.load(sr_t.at[:, :, mine], sr_v.at[:, c]), net.send(sr_t.at[:, :, theirs], sr_v.at[:, c], c=1)

    def student(copies):
        for copy in copies:
            copy.wait_recv()
        so_v[...] = sr_v[...].reshape(4, 320, 256).astype(F32) + jnp.dot(
            s_v[...].reshape(1280, 2048), ws_v[...].reshape(2048, 256), preferred_element_type=F32
        ).reshape(4, 320, 256)

    def transpose():
        load_s.wait()
        for copy in s_pair:
            copy.wait_recv()

        @pl.loop(0, 8)
        def _(j):
            cols = pl.ds(pl.multiple_of(j * 256, 256), 256)
            st_v[cols] = s_v[:, :, :, cols].reshape(1280, 256).T

    load_a.wait()
    t_v[...] = jnp.zeros_like(t_v)
    products(2)
    pl.semaphore_wait(barrier, len(partners))
    p_x = plane_x()
    ws_z = [net.send(ws_in.at[:, slab(step(z, by))], ws_t.at[z], z=by) for by in (1, 3, 2)]
    x_far(2)
    products(3)
    y_first_send(3, 1)
    y_first_send(3, 3)
    sr_z = [net.send(sr_in.at[:, slab(step(z, by))], sr_t.at[z], z=by) for by in (1, 3, 2)]
    y_first_send(3, 2)
    products(6)
    products(7)
    x_direct(2)
    products(1)
    x_relay(2)
    sr_copies = sr_end()
    w_pair = ws_pair()
    y_first_send(3, 0)
    x_far(1)
    p_ring = plane_y(p_x, p_at)
    y_first_direct(3)
    y_first_send(7, 0)
    products(0)
    y_first_far(3)
    y_first_send(7, 2)
    products(4)
    s_ring = {by: net.send(s_in, s_v.at[z, c], z=by) for by in (1, 3)}
    s_pair = [net.send(s_in, s_v.at[z, c], c=1)]
    x_far(0)
    x_far(4)
    y_first_send(7, 1)
    x_far(6)
    x_relay(1)
    x_direct(6)
    x_direct(1)
    x_sum(2)
    load_r.wait()
    y_sum(2)
    products(5)
    x_relay(0)
    x_sum(1)
    s_sends = s_on()
    y_first_relay(3)
    x_direct(0)
    y_sum(1)
    x_relay(6)
    x_direct(4)
    y_first_send(7, 3)
    x_sum(0)
    x_relay(4)
    p_on = plane_y_on(p_ring, p_at)
    hg_on(1)
    y_first_out(3)
    s_end(s_sends)
    x_far(5)
    hg_on(2)
    x_sum(6)
    w_x = ws_x(w_pair)
    y_sum(0)
    x_sum(4)
    y_first_far(7)
    x_direct(5)
    hg_on(3)
    y_sum(6)
    x_relay(5)
    y_sum(4)
    hg_end(3)
    ws_ring = plane_y(w_x, ws_at)
    hg_on(6)
    transpose()
    hg_end(1)
    y_first_direct(7)
    x_sum(5)
    hg_on(0)
    y_first_relay(7)
    hg_end(6)
    hg_end(2)
    hg_on(4)
    y_first_out(7)
    ws_on = plane_y_on(ws_ring, ws_at)
    hg_end(4)
    y_sum(5)
    inverse = lax.rsqrt(sum(squares) * (1.0 / 4096.0) + 1e-05)
    iv_v[z, c] = jnp.broadcast_to(inverse, (160, 128)).T[:8]
    iv_z = [net.send(iv_v.at[z, c], iv_v.at[z, c], z=by) for by in (1, 3, 2)]
    sr_copies[0].wait()
    student(ws_on + [sr_copies[1]])
    hg_end(0)
    hg_on(7)
    for copy in p_on:
        copy.wait_recv()
    hg_dot(6)
    hg_on(5)
    hg_dot(2)
    hg_dot(1)
    hg_dot(4)
    hg_end(7)
    hg_dot(0)
    for copy in iv_z:
        copy.wait_recv()
    iv_pair = net.send(iv_v.at[:, c], iv_v.at[:, c], c=1)
    hg_end(5)
    hg_dot(3)
    hg_dot(7)
    hg_dot(5)
    iv_pair.wait_recv()
    for i in range(4):
        for core in range(2):
            scale = iv_v[i, core].T[:, 0:1]
            rows = pl.ds(core * 160, 160)
            g_v[i, rows] = (128.0 / 20480.0 * (so_v[i, rows] - scale * t_v[i, rows])).astype(BF16)

    @pl.loop(0, 2)
    def _(i):
        rows = pl.ds(pl.multiple_of(i * 1024, 1024), 1024)
        res = jnp.dot(st_v[rows], g_v[...].reshape(1280, 256), preferred_element_type=F32)
        grad[i] = res.astype(BF16).reshape(4, 2, 4, 2, 16, 256)

    left, right = pl.ds(0, 128), pl.ds(128, 128)
    first_x = [net.send(grad.at[:, :, :, step(x, by), :, :, left], ga1.at[by - 1], x=by) for by in (1, 3, 2)]
    first_y = []
    for by in (1, 3, 2):
        to = step(y, by)
        ref = grad.at[lax.rem(to, 2), :, :, :, lax.div(to, 2), :, right]
        first_y.append(net.send(ref, gb1.at[by - 1], y=by))
    for copy in first_x:
        copy.wait_recv()
    total = grad[:, :, :, x, :, :, left].astype(F32)
    ga2[...] = total + ga1[0].astype(F32) + ga1[1].astype(F32) + ga1[2].astype(F32)
    second_y = []
    for by in (1, 3, 2):
        to = step(y, by)
        second_y.append(net.send(ga2.at[lax.rem(to, 2), :, :, lax.div(to, 2)], ra2.at[by - 1], y=by))
    for copy in first_y:
        copy.wait_recv()
    total = grad[yl, :, :, :, yh, :, right].astype(F32)
    gb2[...] = total + gb1[0].astype(F32) + gb1[1].astype(F32) + gb1[2].astype(F32)
    second_x = [net.send(gb2.at[:, :, step(x, by)], rb2.at[by - 1], x=by) for by in (1, 3, 2)]
    for copy in second_y:
        copy.wait_recv()
    fin[:, :, :, left] = ga2[yl, :, :, yh] + ra2[0] + ra2[1] + ra2[2]
    for copy in second_x:
        copy.wait_recv()
    fin[:, :, :, right] = gb2[:, :, x] + rb2[0] + rb2[1] + rb2[2]

    last = []
    for by, core in ((0, 1), (1, 0), (3, 0), (1, 1), (3, 1), (2, 0), (2, 1)):
        ref = fin.at[step(z, by), lax.rem(c + core, 2)]
        last.append(net.send(ref, o_r.at[z, c], z=by, c=core))
    o_r[z, c] = fin[z, c]
    for copy in last:
        copy.wait_recv()
    for i in range(4):
        for core in range(2):
            out[:, pl.ds(i * 512 + core * 256, 256)] = o_r[i, core]

    for copy in net.sent:
        copy.wait_send()


def per_device(a, w, resid, gain, projector, s, s_resid, ws):
    anywhere = pl.BlockSpec(memory_space=pl.ANY)
    vmem = pl.BlockSpec(memory_space=pltpu.VMEM)
    chunks = 4096 // WIDE
    return pl.pallas_call(
        kernel,
        out_shape=jax.ShapeDtypeStruct((16, 2048), F32),
        in_specs=[anywhere, anywhere, anywhere, vmem, anywhere, anywhere, anywhere, anywhere],
        out_specs=vmem,
        scratch_shapes=[
            pltpu.VMEM((4, 320, 1024), BF16),
            pltpu.VMEM((2, 1024, WIDE), BF16),
            pltpu.VMEM((chunks, 4, 2, 160, WIDE), BF16),
            pltpu.VMEM((chunks, 2, 160, WIDE), BF16),
            pltpu.VMEM((chunks, 2, 2, 160, WIDE), BF16),
            pltpu.VMEM((chunks, 160, WIDE), BF16),
            pltpu.VMEM((len(Y_FIRST), 4, 160, WIDE), BF16),
            pltpu.VMEM((160, 4096), BF16),
            pltpu.VMEM((chunks, 4, 2, 160, WIDE), BF16),
            pltpu.VMEM((4, 2, 2, 256, 256), BF16),
            pltpu.VMEM((4, 16, 512), BF16),
            pltpu.VMEM((2, 4, 2, 4, 2, 16, 256), BF16),
            pltpu.VMEM((4, 2, 160, 2048), BF16),
            pltpu.VMEM((2048, 1280), BF16),
            pltpu.VMEM((4, 160, 512), BF16),
            pltpu.VMEM((4, 2, 160, 256), BF16),
            pltpu.VMEM((4, 320, 256), F32),
            pltpu.VMEM((4, 320, 256), F32),
            pltpu.VMEM((4, 320, 256), BF16),
            pltpu.VMEM((4, 2, 8, 160), F32),
            pltpu.VMEM((2, 4, 2, 4, 2, 16, 256), BF16),
            pltpu.VMEM((3, 2, 4, 2, 2, 16, 128), BF16),
            pltpu.VMEM((3, 4, 2, 4, 16, 128), BF16),
            pltpu.VMEM((2, 4, 2, 2, 16, 128), F32),
            pltpu.VMEM((4, 2, 4, 16, 128), F32),
            pltpu.VMEM((3, 4, 2, 16, 128), F32),
            pltpu.VMEM((3, 4, 2, 16, 128), F32),
            pltpu.VMEM((4, 2, 16, 256), F32),
            pltpu.VMEM((4, 2, 16, 256), F32),
            pltpu.SemaphoreType.DMA((N_SEM,)),
            pltpu.SemaphoreType.DMA((N_SEM,)),
            pltpu.SemaphoreType.DMA((N_LOCAL,)),
        ],
        compiler_params=pltpu.CompilerParams(
            collective_id=0, has_side_effects=True, vmem_limit_bytes=62 * 2**20
        ),
        cost_estimate=pl.CostEstimate(flops=16 * 10**9, bytes_accessed=16 * 10**6, transcendentals=160),
    )(
        a.reshape(4, 320, 1024),
        w,
        resid,
        gain.reshape(1, 4096),
        projector.reshape(2, 256, 2048),
        s,
        s_resid,
        ws,
    )


def solution(mesh):
    return jax.shard_map(
        per_device,
        mesh=mesh,
        in_specs=(
            P("dp", "tensor"),
            P("tensor", None),
            P(("dp", "tensor"), None),
            P(),
            P("tensor", None),
            P(("dp", "tensor"), None),
            P(("dp", "tensor"), None),
            P(("dp", "tensor"), None),
        ),
        out_specs=P(("dp", "tensor"), None),
        check_vma=False,
    )
```

time: 1160 us -> 137 us (0.12)
  waiting for transfers between devices: 1060 us -> 0 us
  Pallas kernels: 0 us -> 136 us
  matrix products: 34.2 us -> 0 us
  blocking collectives: 21.8 us -> 0 us
  local copies, waits for them, and re-layouts: 19.5 us -> 1.57 us
  between operations: 14.9 us -> 0.01 us
    reduce_scatter x3 -> x0, waiting for transfers between devices: 808 us -> none  [the longest x1 670 us: per_device(): lax.psum_scatter(lax.dot_general(columns, out_grad, (((0,), (0,)), ((), (...]
    all_gather x1 -> x0, waiting for transfers between devices: 251 us -> none  [per_device(): lax.all_gather(student_weight, ('dp', 'tensor'), axis=0, tiled=True)]
    pallas_call x0 -> x1, Pallas kernels: none -> 136 us  [per_device(): pl.pallas_call(kernel, out_shape=jax.ShapeDtypeStruct((16, 2048), F32), i...]
    dot_general x3 -> x0, matrix products: 34.2 us -> none  [the longest x1 16.5 us: per_device(): jnp.dot(block_rows, teacher_out_weight, preferred_element_type=jnp.float32)]
    all_to_all x1 -> x0, blocking collectives: 21.8 us -> none  [per_device(): lax.all_to_all(normed, 'tensor', split_axis=1, concat_axis=0, tiled=True)]
    unnamed x17 -> x1, local copies, waits for them, and re-layouts: 19.4 us -> 1.57 us
  transfers between devices with their start and end apart: 4 -> 0, of which waited for: 3 -> 0; matrix products, arithmetic and copies ran while one was open for 1% -> 0% of each run, Pallas kernels for 0% -> 0%
where the time goes in v2:
time: 137 us
  Pallas kernels  136 us (99%)
  local copies, waits for them, and re-layouts  1.57 us (1%)
    pallas_call x1, Pallas kernels, per_device(): pl.pallas_call(kernel, out_shape=jax.ShapeDtypeStruct((16, 2048), F32), i...  136 us

profile of v2, /device:TPU:1, one launch (start us, length us, event | category | flops | bytes accessed | tf_op | source)
XLA Modules:
  0.0 137.1 jit_solution(16520212443282179117)
XLA Ops:
  0.0 135.5 %shard_map.82 = f32[16,2048]{1,0:T(8,128)} custom-call(bf16[4,320,1024]{2,1,0:T(8,128)(2,1)} %bitcast.3, bf16[1024,4096]{1,0:T(8,128)(2,1)} %w_in.1, bf16[160,4096]{1,0:T(8,128)(2,1)} %r_in.1, f32[1,4096]{1,0:T(1,128)} %bitcast.5, bf16[2,256,2048]{2,1,0:T(8,128)(2,1)} %bitcast.4, bf16[160,2048]{1,0:T(8,128)(2,1)} %s_in.1, bf16[160,2048]{1,0:T(8,128)(2,1)} %sr_in.1, ...), custom_call_target="tpu_custom_call" | custom-call | flops 16000000000 | bytes 16000000 | tf_op jit(solution)/shard_map/pallas_call | solution.py:471
  135.5 1.6 %copy.10 = f32[16,2048]{1,0:T(8,128)} copy(f32[16,2048]{1,0:T(8,128)} %shard_map.82) | data formatting | bytes 262144

commit v3 on v0

v3 whole, which is shorter than its diff:
```python
import math

import jax
import jax.numpy as jnp
from jax import lax
from jax.experimental import pallas as pl
from jax.experimental.pallas import tpu as pltpu
from jax.sharding import PartitionSpec as P

MESH = pl.DeviceIdType.MESH
BF16 = jnp.bfloat16
F32 = jnp.float32

WIDE = 512
STARTS = (0, 512, 1024, 1536, 2048, 2560, 3072, 3584)
WIDTHS = (512, 512, 512, 512, 512, 512, 512, 512)
Y_FIRST = (3, 7)
W_ORDER = (5, 3, 1, 6, 0, 7, 2, 4)
N_SEND = 14
N_RECV = 76
N_LOCAL = 16


def step(v, by):
    return lax.rem(v + by, 4)


def factors(tiles):
    for rows in range(64, 0, -1):
        if tiles % rows == 0 and tiles // rows <= 32:
            return rows, tiles // rows
    return None


class Net:
    def __init__(self, send_sems, recv_sems, local_sems, ruler):
        dp, t = lax.axis_index("dp"), lax.axis_index("tensor")
        self.x = lax.div(t, 2)
        self.y = lax.rem(t, 2) * 2 + lax.div(dp, 8)
        self.z = lax.rem(lax.div(dp, 2), 4)
        self.c = lax.rem(dp, 2)
        self.send_sems, self.recv_sems, self.local_sems = send_sems, recv_sems, local_sems
        self.ruler = ruler
        self.used_local = 0
        self.keys = {}
        self.sizes = []

    def at(self, x=0, y=0, z=0, c=0):
        px, py, pz = step(self.x, x), step(self.y, y), step(self.z, z)
        pc = lax.rem(self.c + c, 2)
        return (lax.rem(py, 2) * 8 + pz * 2 + pc, px * 2 + lax.div(py, 2))

    def send(self, key, src, dst, **where):
        tiles = math.prod(src.shape) * src.dtype.itemsize // 4096
        index, total = self.keys.get(key, (len(self.keys), 0))
        self.keys[key] = (index, total + tiles)
        for i, (size, count) in enumerate(self.sizes):
            if size == tiles and factors(size * (count + 1)):
                self.sizes[i] = (size, count + 1)
                break
        else:
            i = len(self.sizes)
            self.sizes.append((tiles, 1))
        pltpu.make_async_remote_copy(
            src_ref=src,
            dst_ref=dst,
            send_sem=self.send_sems.at[i],
            recv_sem=self.recv_sems.at[index],
            device_id=self.at(**where),
            device_id_type=MESH,
        ).start()

    def wait_tiles(self, tiles, sem):
        rows, cols = factors(tiles)
        ref = self.ruler.at[pl.ds(0, rows * 16), pl.ds(0, cols * 128)]
        pltpu.make_async_copy(ref, ref, sem).wait()

    def wait(self, key):
        index, tiles = self.keys[key]
        self.wait_tiles(tiles, self.recv_sems.at[index])

    def wait_sent(self):
        for i, (size, count) in enumerate(self.sizes):
            self.wait_tiles(size * count, self.send_sems.at[i])

    def load(self, src, dst):
        i = self.used_local
        self.used_local += 1
        copy = pltpu.make_async_copy(src, dst, self.local_sems.at[i])
        copy.start()
        return copy


def kernel(
    a_in, w_in, r_in, gain, p_in, s_in, sr_in, ws_in, out,
    a_v, w_v, c_v, ra, rb, ry, ry4, r_v, hg_v, p_v, ws_t, ws_v, s_v, st_v, sr_t, sr_v, t_v, so_v, g_v,
    iv_v, grad, ga1, gb1, ga2, gb2, ra2, rb2, fin, o_r,
    send_sems, recv_sems, local_sems,
):
    net = Net(send_sems, recv_sems, local_sems, w_in)
    x, y, z, c = net.x, net.y, net.z, net.c
    other_c = 1 - c
    yh, yl = lax.div(y, 2), lax.rem(y, 2)
    other_yh = 1 - yh
    my_cols = pl.ds(pl.multiple_of(z * 512 + c * 256, 256), 256)
    mine = pl.ds(pl.multiple_of(c * 256, 256), 256)
    theirs = pl.ds(pl.multiple_of(other_c * 256, 256), 256)

    def slab(zv):
        return pl.ds(pl.multiple_of(zv * 512, 512), 512)

    load_a = net.load(a_in, a_v)
    w_loads = {}

    def load_w(n):
        if n < len(W_ORDER):
            k = W_ORDER[n]
            cols = pl.ds(STARTS[k], WIDTHS[k])
            w_loads[n] = net.load(w_in.at[:, cols], w_v.at[n % 2, :, pl.ds(0, WIDTHS[k])])

    load_w(0)

    partners = [dict(c=1)] + [{axis: by} for axis in "xyz" for by in (1, 2, 3)] + [dict(z=by, c=1) for by in (1, 2, 3)]
    barrier = pltpu.get_barrier_semaphore()
    for where in partners:
        pl.semaphore_signal(barrier, inc=1, device_id=net.at(**where), device_id_type=MESH)

    def ahead(by):
        return step(x, by)

    def products(k):
        n = W_ORDER.index(k)
        w_loads[n].wait()

        @pl.loop(0, WIDTHS[k] // 256)
        def _(j):
            cols = pl.ds(pl.multiple_of(j * 256, 256), 256)
            res = jnp.dot(a_v[...].reshape(1280, 1024), w_v[n % 2, :, cols], preferred_element_type=F32)
            c_v[k, :, :, :, cols] = res.astype(BF16).reshape(4, 2, 160, 256)

        load_w(n + 2)

    low, high = pl.ds(0, 80), pl.ds(80, 80)

    def block(ref, *index, rows=pl.ds(0, 160)):
        return ref.at[(*index, rows, pl.ds(0, WIDTHS[index[0]]))]

    def read(ref, *index, rows=pl.ds(0, 160)):
        return block(ref, *index, rows=rows)[...].astype(F32)

    def write(value, ref, *index, rows=pl.ds(0, 160)):
        block(ref, *index, rows=rows)[...] = value.astype(BF16)

    def x_far(k):
        net.send(("far", k), block(c_v, k, ahead(2), 0), block(ra, k, 0), x=1)
        net.send(("far", k), block(c_v, k, ahead(2), 1), block(ra, k, 1), x=3)

    def x_direct(k):
        net.send(("near", k), block(c_v, k, ahead(1), 1), block(rb, k, 0, 1), x=1)
        net.send(("near", k), block(c_v, k, ahead(3), 0), block(rb, k, 1, 0), x=3)

    def x_relay(k):
        net.wait(("far", k))
        for way, rel, by in ((0, 1, 1), (1, 3, 3)):
            to = ahead(rel)
            write(read(c_v, k, to, way) + read(ra, k, way), c_v, k, to, way)
            net.send(("near", k), block(c_v, k, to, way), block(rb, k, way, way), x=by)

    def x_total(k, h):
        return read(c_v, k, x, h) + read(rb, k, 0, h) + read(rb, k, 1, h)

    def x_sum(k):
        net.wait(("near", k))
        write(x_total(k, other_yh), c_v, k, x, other_yh)
        net.send(("y", k), block(c_v, k, x, other_yh), block(ry, k), y=2)

    squares = []

    def hidden_out(k, attended):
        cols = pl.ds(STARTS[k], WIDTHS[k])
        hidden = r_v[:, cols].astype(F32) + attended
        squares.append(jnp.sum(hidden * hidden, axis=-1, keepdims=True))
        write(hidden * gain[:, cols], hg_v, k, z, c)
        ref = block(hg_v, k, z, c)
        for by in (1, 3):
            net.send(("hg", k), ref, ref, z=by)
        net.send(("pair", k), ref, ref, c=1)

    def y_sum(k):
        net.wait(("y", k))
        hidden_out(k, x_total(k, yh) + read(ry, k))

    def y_first_send(k, rel):
        ref = ry4.at[Y_FIRST.index(k), rel, :, pl.ds(0, WIDTHS[k])]
        net.send(("y", k, rel), block(c_v, k, ahead(rel), other_yh), ref, y=2)

    def y_first_add(k, rel):
        net.wait(("y", k, rel))
        ref = ry4.at[Y_FIRST.index(k), rel, :, pl.ds(0, WIDTHS[k])]
        write(read(c_v, k, ahead(rel), yh) + ref[...].astype(F32), c_v, k, ahead(rel), yh)

    def y_first_far(k):
        y_first_add(k, 2)
        net.send(("far", k), block(c_v, k, ahead(2), yh, rows=low), block(ra, k, 0, rows=low), x=1)
        net.send(("far", k), block(c_v, k, ahead(2), yh, rows=high), block(ra, k, 1, rows=high), x=3)

    def y_first_direct(k):
        y_first_add(k, 1)
        net.send(("near", k), block(c_v, k, ahead(1), yh, rows=high), block(rb, k, 0, 0, rows=high), x=1)
        y_first_add(k, 3)
        net.send(("near", k), block(c_v, k, ahead(3), yh, rows=low), block(rb, k, 1, 0, rows=low), x=3)

    def y_first_relay(k):
        net.wait(("far", k))
        for way, rel, by, rows in ((0, 1, 1, low), (1, 3, 3, high)):
            to = ahead(rel)
            write(read(c_v, k, to, yh, rows=rows) + read(ra, k, way, rows=rows), c_v, k, to, yh, rows=rows)
            net.send(("near", k), block(c_v, k, to, yh, rows=rows), block(rb, k, way, 0, rows=rows), x=by)

    def y_first_out(k):
        y_first_add(k, 0)
        net.wait(("near", k))
        hidden_out(k, read(c_v, k, x, yh) + read(rb, k, 0, 0) + read(rb, k, 1, 0))

    def hg_on(k):
        net.wait(("hg", k))
        for by, rows in ((1, low), (3, high)):
            source = step(z, 4 - by)
            ref = block(hg_v, k, source, c, rows=rows)
            net.send(("on", k), ref, ref, z=by)
        for by in (1, 3):
            ref = block(hg_v, k, step(z, 4 - by), c)
            net.send(("pair", k), ref, ref, c=1)

    def hg_end(k):
        net.wait(("on", k))
        ref = block(hg_v, k, step(z, 2), c)
        net.send(("pair", k), ref, ref, c=1)

    def hg_dot(k):
        net.wait(("pair", k))
        start, width = STARTS[k], WIDTHS[k]
        shard = start // 512
        halves = p_v[shard // 2, shard % 2]
        if width == 256:
            halves = halves[start % 512 // 256]
        t_v[...] += jnp.dot(
            hg_v[k, :, :, :, :width].reshape(1280, width),
            halves.reshape(width, 256),
            preferred_element_type=F32,
        ).reshape(4, 320, 256)

    begins = ((1, pl.ds(0, 128)), (3, pl.ds(128, 128)))

    def p_x():
        for by in (1, 3):
            net.send("p_x", p_in.at[yl, :, my_cols], p_v.at[x, yh, yl], x=by)

    def p_x_on():
        net.wait("p_x")
        for by, cols in begins:
            ref = p_v.at[step(x, 4 - by), yh, yl, :, cols]
            net.send("p_x_on", ref, ref, x=by)

    def p_at(yv, cols):
        return p_v.at[:, lax.div(yv, 2), lax.rem(yv, 2), :, cols]

    def p_ring():
        load_p.wait()
        net.wait("p_x_on")
        ref = p_at(y, pl.ds(0, 256))
        for by in (1, 3):
            net.send("p_ring", ref, ref, y=by)

    def p_on():
        net.wait("p_ring")
        for by, cols in begins:
            ref = p_at(step(y, 4 - by), cols)
            net.send("p_on", ref, ref, y=by)

    def ws_z():
        for by in (1, 3, 2):
            net.send("ws_z", ws_in.at[:, slab(step(z, by))], ws_t.at[z], z=by)

    def w_pair():
        load_ws.wait()
        net.wait("ws_z")
        net.send("w_pair", ws_t.at[:, :, theirs], ws_v.at[yl, :, c, x, yh], c=1)
        return net.load(ws_t.at[:, :, mine], ws_v.at[yl, :, c, x, yh])

    def w_x(copy):
        copy.wait()
        net.wait("w_pair")
        ref = ws_v.at[yl, :, :, x, yh]
        for by in (1, 3):
            net.send("w_x", ref, ref, x=by)

    def w_x_on():
        net.wait("w_x")
        for by, cols in begins:
            ref = ws_v.at[yl, :, :, step(x, 4 - by), yh, :, cols]
            net.send("w_x_on", ref, ref, x=by)

    def ws_at(yv, cols):
        return ws_v.at[lax.rem(yv, 2), :, :, :, lax.div(yv, 2), :, cols]

    def ws_ring():
        net.wait("w_x_on")
        ref = ws_at(y, pl.ds(0, 256))
        for by in (1, 3):
            net.send("ws_ring", ref, ref, y=by)

    def ws_on():
        net.wait("ws_ring")
        for by, cols in begins:
            ref = ws_at(step(y, 4 - by), cols)
            net.send("ws_on", ref, ref, y=by)

    def s_ring():
        for by in (1, 3):
            net.send("s_ring", s_in, s_v.at[z, c], z=by)
        net.send("s_pair", s_in, s_v.at[z, c], c=1)

    def s_on():
        net.wait("s_ring")
        for by, rows in ((1, low), (3, high)):
            ref = s_v.at[step(z, 4 - by), c, rows]
            net.send("s_on", ref, ref, z=by)
        for by in (1, 3):
            ref = s_v.at[step(z, 4 - by), c]
            net.send("s_pair", ref, ref, c=1)

    def s_end():
        net.wait("s_on")
        ref = s_v.at[step(z, 2), c]
        net.send("s_pair", ref, ref, c=1)

    def sr_z():
        for by in (1, 3, 2):
            net.send("sr_z", sr_in.at[:, slab(step(z, by))], sr_t.at[z], z=by)

    def sr_end():
        load_sr.wait()
        net.wait("sr_z")
        net.send("sr_pair", sr_t.at[:, :, theirs], sr_v.at[:, c], c=1)
        return net.load(sr_t.at[:, :, mine], sr_v.at[:, c])

    def transpose():
        load_s.wait()
        net.wait("s_pair")

        @pl.loop(0, 8)
        def _(j):
            cols = pl.ds(pl.multiple_of(j * 256, 256), 256)
            st_v[cols] = s_v[:, :, :, cols].reshape(1280, 256).T

    def student(copy):
        copy.wait()
        net.wait("sr_pair")
        net.wait("ws_on")
        so_v[...] = sr_v[...].reshape(4, 320, 256).astype(F32) + jnp.dot(
            s_v[...].reshape(1280, 2048), ws_v[...].reshape(2048, 256), preferred_element_type=F32
        ).reshape(4, 320, 256)

    pl.semaphore_wait(barrier, len(partners))
    p_x()
    ws_z()
    s_ring()
    load_a.wait()
    load_w(1)
    load_p = net.load(p_in.at[yl, :, my_cols], p_v.at[x, yh, yl])
    load_ws = net.load(ws_in.at[:, slab(z)], ws_t.at[z])
    load_sr = net.load(sr_in.at[:, slab(z)], sr_t.at[z])
    load_s = net.load(s_in, s_v.at[z, c])
    load_r = net.load(r_in, r_v)
    t_v[...] = jnp.zeros_like(t_v)
    products(5)
    x_direct(5)
    products(3)
    products(1)
    x_far(5)
    p_x_on()
    x_far(1)
    y_first_send(3, 1)
    y_first_send(3, 2)
    products(6)
    products(0)
    products(7)
    x_far(0)
    y_first_send(3, 0)
    y_first_send(3, 3)
    y_first_send(7, 1)
    x_direct(1)
    y_first_send(7, 2)
    x_relay(1)
    products(2)
    sr_z()
    y_first_far(3)
    x_relay(5)
    y_first_direct(3)
    p_ring()
    x_sum(5)
    x_far(6)
    y_first_send(7, 3)
    s_on()
    w_copy = w_pair()
    y_first_relay(3)
    y_first_far(7)
    x_direct(0)
    x_sum(1)
    load_r.wait()
    y_first_out(3)
    x_relay(0)
    w_x(w_copy)
    x_far(2)
    hg_on(3)
    x_relay(6)
    y_sum(1)
    products(4)
    y_first_direct(7)
    y_first_send(7, 0)
    p_on()
    y_sum(5)
    x_relay(2)
    x_sum(0)
    x_direct(2)
    y_first_relay(7)
    hg_on(1)
    hg_end(1)
    hg_on(5)
    y_first_out(7)
    w_x_on()
    x_direct(6)
    x_sum(2)
    hg_end(5)
    y_sum(0)
    x_far(4)
    x_sum(6)
    hg_on(7)
    x_direct(4)
    hg_end(3)
    net.wait("p_on")
    hg_dot(1)
    y_sum(2)
    s_end()
    ws_ring()
    x_relay(4)
    hg_on(0)
    y_sum(6)
    x_sum(4)
    sr_copy = sr_end()
    hg_end(0)
    hg_dot(5)
    transpose()
    hg_end(7)
    hg_on(2)
    hg_on(6)
    hg_dot(3)
    y_sum(4)
    hg_end(2)
    ws_on()
    hg_dot(2)
    hg_end(6)
    hg_dot(7)
    hg_dot(0)
    inverse = lax.rsqrt(sum(squares) * (1.0 / 4096.0) + 1e-05)
    iv_v[z, c, :, 0:160] = jnp.broadcast_to(inverse, (160, 128)).T[:8]
    for by in (1, 3, 2):
        net.send("scale", iv_v.at[z, c], iv_v.at[z, c], z=by)
    hg_on(4)
    student(sr_copy)
    hg_end(4)
    hg_dot(6)
    net.wait("scale")
    net.send("scale_pair", iv_v.at[:, c], iv_v.at[:, c], c=1)
    hg_dot(4)
    net.wait("scale_pair")
    for i in range(4):
        for core in range(2):
            scale = iv_v[i, core, :, 0:160].T[:, 0:1]
            rows = pl.ds(core * 160, 160)
            g_v[i, rows] = (128.0 / 20480.0 * (so_v[i, rows] - scale * t_v[i, rows])).astype(BF16)

    left, right = pl.ds(0, 128), pl.ds(128, 128)
    for half, near in ((1 - yl, (1, 3)), (yl, (2,))):
        rows = pl.ds(pl.multiple_of(half * 1024, 1024), 1024)
        res = jnp.dot(st_v[rows], g_v[...].reshape(1280, 256), preferred_element_type=F32)
        grad[half] = res.astype(BF16).reshape(4, 2, 4, 2, 16, 256)
        for by in near:
            ref = grad.at[half, :, :, :, lax.div(step(y, by), 2), :, right]
            net.send("y_1", ref, gb1.at[by - 1], y=by)
        for by in (1, 3, 2):
            net.send("x_1", grad.at[half, :, :, step(x, by), :, :, left], ga1.at[by - 1, half], x=by)

    def four(own, others):
        return own.astype(F32) + others[0].astype(F32) + others[1].astype(F32) + others[2].astype(F32)

    net.wait("x_1")
    ga2[...] = four(grad[:, :, :, x, :, :, left], ga1).astype(BF16)
    for by in (1, 3, 2):
        to = step(y, by)
        net.send("y_2", ga2.at[lax.rem(to, 2), :, :, lax.div(to, 2)], ra2.at[by - 1], y=by)
    net.wait("y_1")
    gb2[...] = four(grad[yl, :, :, :, yh, :, right], gb1).astype(BF16)
    for by in (1, 3, 2):
        net.send("x_2", gb2.at[:, :, step(x, by)], rb2.at[by - 1], x=by)
    net.wait("y_2")
    fin[:, :, :, left] = four(ga2[yl, :, :, yh], ra2)
    net.wait("x_2")
    fin[:, :, :, right] = four(gb2[:, :, x], rb2)

    for by, core in ((0, 1), (1, 0), (3, 0), (1, 1), (3, 1), (2, 0), (2, 1)):
        ref = fin.at[step(z, by), lax.rem(c + core, 2)]
        net.send("rows", ref, o_r.at[z, c], z=by, c=core)
    o_r[z, c] = fin[z, c]
    net.wait("rows")
    for i in range(4):
        for core in range(2):
            out[:, pl.ds(i * 512 + core * 256, 256)] = o_r[i, core]

    net.wait_sent()


def per_device(a, w, resid, gain, projector, s, s_resid, ws):
    anywhere = pl.BlockSpec(memory_space=pl.ANY)
    vmem = pl.BlockSpec(memory_space=pltpu.VMEM)
    chunks = len(WIDTHS)
    return pl.pallas_call(
        kernel,
        out_shape=jax.ShapeDtypeStruct((16, 2048), F32),
        in_specs=[anywhere, anywhere, anywhere, vmem, anywhere, anywhere, anywhere, anywhere],
        out_specs=vmem,
        scratch_shapes=[
            pltpu.VMEM((4, 320, 1024), BF16),
            pltpu.VMEM((2, 1024, WIDE), BF16),
            pltpu.VMEM((chunks, 4, 2, 160, WIDE), BF16),
            pltpu.VMEM((chunks, 2, 160, WIDE), BF16),
            pltpu.VMEM((chunks, 2, 2, 160, WIDE), BF16),
            pltpu.VMEM((chunks, 160, WIDE), BF16),
            pltpu.VMEM((len(Y_FIRST), 4, 160, WIDE), BF16),
            pltpu.VMEM((160, 4096), BF16),
            pltpu.VMEM((chunks, 4, 2, 160, WIDE), BF16),
            pltpu.VMEM((4, 2, 2, 256, 256), BF16),
            pltpu.VMEM((4, 16, 512), BF16),
            pltpu.VMEM((2, 4, 2, 4, 2, 16, 256), BF16),
            pltpu.VMEM((4, 2, 160, 2048), BF16),
            pltpu.VMEM((2048, 1280), BF16),
            pltpu.VMEM((4, 160, 512), BF16),
            pltpu.VMEM((4, 2, 160, 256), BF16),
            pltpu.VMEM((4, 320, 256), F32),
            pltpu.VMEM((4, 320, 256), F32),
            pltpu.VMEM((4, 320, 256), BF16),
            pltpu.VMEM((4, 2, 8, 256), F32),
            pltpu.VMEM((2, 4, 2, 4, 2, 16, 256), BF16),
            pltpu.VMEM((3, 2, 4, 2, 2, 16, 128), BF16),
            pltpu.VMEM((3, 4, 2, 4, 16, 128), BF16),
            pltpu.VMEM((2, 4, 2, 2, 16, 128), BF16),
            pltpu.VMEM((4, 2, 4, 16, 128), BF16),
            pltpu.VMEM((3, 4, 2, 16, 128), BF16),
            pltpu.VMEM((3, 4, 2, 16, 128), BF16),
            pltpu.VMEM((4, 2, 16, 256), F32),
            pltpu.VMEM((4, 2, 16, 256), F32),
            pltpu.SemaphoreType.DMA((N_SEND,)),
            pltpu.SemaphoreType.DMA((N_RECV,)),
            pltpu.SemaphoreType.DMA((N_LOCAL,)),
        ],
        compiler_params=pltpu.CompilerParams(
            collective_id=0, has_side_effects=True, vmem_limit_bytes=62 * 2**20
        ),
        cost_estimate=pl.CostEstimate(flops=16 * 10**9, bytes_accessed=16 * 10**6, transcendentals=160),
    )(
        a.reshape(4, 320, 1024),
        w,
        resid,
        gain.reshape(1, 4096),
        projector.reshape(2, 256, 2048),
        s,
        s_resid,
        ws,
    )


def solution(mesh):
    return jax.shard_map(
        per_device,
        mesh=mesh,
        in_specs=(
            P("dp", "tensor"),
            P("tensor", None),
            P(("dp", "tensor"), None),
            P(),
            P("tensor", None),
            P(("dp", "tensor"), None),
            P(("dp", "tensor"), None),
            P(("dp", "tensor"), None),
        ),
        out_specs=P(("dp", "tensor"), None),
        check_vma=False,
    )
```

time: 1160 us -> 131 us (0.11)
  waiting for transfers between devices: 1060 us -> 0 us
  Pallas kernels: 0 us -> 130 us
  matrix products: 34.2 us -> 0 us
  blocking collectives: 21.8 us -> 0 us
  local copies, waits for them, and re-layouts: 19.5 us -> 1.57 us
  between operations: 14.9 us -> 0.01 us
    reduce_scatter x3 -> x0, waiting for transfers between devices: 808 us -> none  [the longest x1 670 us: per_device(): lax.psum_scatter(lax.dot_general(columns, out_grad, (((0,), (0,)), ((), (...]
    all_gather x1 -> x0, waiting for transfers between devices: 251 us -> none  [per_device(): lax.all_gather(student_weight, ('dp', 'tensor'), axis=0, tiled=True)]
    pallas_call x0 -> x1, Pallas kernels: none -> 130 us  [per_device(): pl.pallas_call(kernel, out_shape=jax.ShapeDtypeStruct((16, 2048), F32), i...]
    dot_general x3 -> x0, matrix products: 34.2 us -> none  [the longest x1 16.5 us: per_device(): jnp.dot(block_rows, teacher_out_weight, preferred_element_type=jnp.float32)]
    all_to_all x1 -> x0, blocking collectives: 21.8 us -> none  [per_device(): lax.all_to_all(normed, 'tensor', split_axis=1, concat_axis=0, tiled=True)]
    unnamed x17 -> x1, local copies, waits for them, and re-layouts: 19.4 us -> 1.57 us
  transfers between devices with their start and end apart: 4 -> 0, of which waited for: 3 -> 0; matrix products, arithmetic and copies ran while one was open for 1% -> 0% of each run, Pallas kernels for 0% -> 0%
where the time goes in v3:
time: 131 us
  Pallas kernels  130 us (99%)
  local copies, waits for them, and re-layouts  1.57 us (1%)
    pallas_call x1, Pallas kernels, per_device(): pl.pallas_call(kernel, out_shape=jax.ShapeDtypeStruct((16, 2048), F32), i...  130 us

profile of v3, /device:TPU:1, one launch (start us, length us, event | category | flops | bytes accessed | tf_op | source)
XLA Modules:
  0.0 131.2 jit_solution(1405459304025983678)
XLA Ops:
  0.0 129.6 %shard_map.82 = f32[16,2048]{1,0:T(8,128)} custom-call(bf16[4,320,1024]{2,1,0:T(8,128)(2,1)} %bitcast.3, bf16[1024,4096]{1,0:T(8,128)(2,1)} %w_in.1, bf16[160,4096]{1,0:T(8,128)(2,1)} %r_in.1, f32[1,4096]{1,0:T(1,128)} %bitcast.5, bf16[2,256,2048]{2,1,0:T(8,128)(2,1)} %bitcast.4, bf16[160,2048]{1,0:T(8,128)(2,1)} %s_in.1, bf16[160,2048]{1,0:T(8,128)(2,1)} %sr_in.1, ...), custom_call_target="tpu_custom_call" | custom-call | flops 16000000000 | bytes 16000000 | tf_op jit(solution)/shard_map/pallas_call | solution.py:528
  129.6 1.6 %copy.10 = f32[16,2048]{1,0:T(8,128)} copy(f32[16,2048]{1,0:T(8,128)} %shard_map.82) | data formatting | bytes 262144

commit v4 on v3

--- a/solution.py
+++ b/solution.py
@@ -358,9 +358,13 @@
         copy.wait()
         net.wait("sr_pair")
         net.wait("ws_on")
-        so_v[...] = sr_v[...].reshape(4, 320, 256).astype(F32) + jnp.dot(
-            s_v[...].reshape(1280, 2048), ws_v[...].reshape(2048, 256), preferred_element_type=F32
-        ).reshape(4, 320, 256)
+
+        @pl.loop(0, 4)
+        def _(i):
+            so_v[i] = sr_v[i].reshape(320, 256).astype(F32) + jnp.dot(
+                s_v[i].reshape(320, 2048), ws_v[...].reshape(2048, 256), preferred_element_type=F32
+            )
+
 
     pl.semaphore_wait(barrier, len(partners))
     p_x()
@@ -483,9 +487,13 @@
 
     left, right = pl.ds(0, 128), pl.ds(128, 128)
     for half, near in ((1 - yl, (1, 3)), (yl, (2,))):
-        rows = pl.ds(pl.multiple_of(half * 1024, 1024), 1024)
-        res = jnp.dot(st_v[rows], g_v[...].reshape(1280, 256), preferred_element_type=F32)
-        grad[half] = res.astype(BF16).reshape(4, 2, 4, 2, 16, 256)
+
+        @pl.loop(0, 2)
+        def _(i):
+            rows = pl.ds(pl.multiple_of(half * 1024 + i * 512, 512), 512)
+            res = jnp.dot(st_v[rows], g_v[...].reshape(1280, 256), preferred_element_type=F32)
+            grad[half, pl.ds(i * 2, 2)] = res.astype(BF16).reshape(2, 2, 4, 2, 16, 256)
+
         for by in near:
             ref = grad.at[half, :, :, :, lax.div(step(y, by), 2), :, right]
             net.send("y_1", ref, gb1.at[by - 1], y=by)

time: 131 us -> 131 us (level)
  no operation moved by 1% of the time
where the time goes in v4:
time: 131 us
  Pallas kernels  129 us (98%)
  local copies, waits for them, and re-layouts  1.57 us (1%)
    pallas_call x1, Pallas kernels, per_device(): pl.pallas_call(kernel, out_shape=jax.ShapeDtypeStruct((16, 2048), F32), i...  129 us

profile of v4, /device:TPU:1, one launch (start us, length us, event | category | flops | bytes accessed | tf_op | source)
XLA Modules:
  0.0 130.6 jit_solution(2471234670244759277)
XLA Ops:
  0.0 129.0 %shard_map.82 = f32[16,2048]{1,0:T(8,128)} custom-call(bf16[4,320,1024]{2,1,0:T(8,128)(2,1)} %bitcast.3, bf16[1024,4096]{1,0:T(8,128)(2,1)} %w_in.1, bf16[160,4096]{1,0:T(8,128)(2,1)} %r_in.1, f32[1,4096]{1,0:T(1,128)} %bitcast.5, bf16[2,256,2048]{2,1,0:T(8,128)(2,1)} %bitcast.4, bf16[160,2048]{1,0:T(8,128)(2,1)} %s_in.1, bf16[160,2048]{1,0:T(8,128)(2,1)} %sr_in.1, ...), custom_call_target="tpu_custom_call" | custom-call | flops 16000000000 | bytes 16000000 | tf_op jit(solution)/shard_map/pallas_call | solution.py:536
  129.0 1.6 %copy.10 = f32[16,2048]{1,0:T(8,128)} copy(f32[16,2048]{1,0:T(8,128)} %shard_map.82) | data formatting | bytes 262144

commit v5 on v4

--- a/solution.py
+++ b/solution.py
@@ -109,6 +109,11 @@
     def slab(zv):
         return pl.ds(pl.multiple_of(zv * 512, 512), 512)
 
+    partners = [{axis: 2} for axis in "xyz"] + [dict(z=by, c=1) for by in (2, 1, 3)] + [{axis: by} for axis in "xyz" for by in (1, 3)] + [dict(c=1)]
+    barrier = pltpu.get_barrier_semaphore()
+    for where in partners:
+        pl.semaphore_signal(barrier, inc=1, device_id=net.at(**where), device_id_type=MESH)
+
     load_a = net.load(a_in, a_v)
     w_loads = {}
 
@@ -119,11 +124,6 @@
             w_loads[n] = net.load(w_in.at[:, cols], w_v.at[n % 2, :, pl.ds(0, WIDTHS[k])])
 
     load_w(0)
-
-    partners = [dict(c=1)] + [{axis: by} for axis in "xyz" for by in (1, 2, 3)] + [dict(z=by, c=1) for by in (1, 2, 3)]
-    barrier = pltpu.get_barrier_semaphore()
-    for where in partners:
-        pl.semaphore_signal(barrier, inc=1, device_id=net.at(**where), device_id_type=MESH)
 
     def ahead(by):
         return step(x, by)
@@ -497,7 +497,7 @@
         for by in near:
             ref = grad.at[half, :, :, :, lax.div(step(y, by), 2), :, right]
             net.send("y_1", ref, gb1.at[by - 1], y=by)
-        for by in (1, 3, 2):
+        for by in (2, 1, 3):
             net.send("x_1", grad.at[half, :, :, step(x, by), :, :, left], ga1.at[by - 1, half], x=by)
 
     def four(own, others):
@@ -505,19 +505,19 @@
 
     net.wait("x_1")
     ga2[...] = four(grad[:, :, :, x, :, :, left], ga1).astype(BF16)
-    for by in (1, 3, 2):
+    for by in (2, 1, 3):
         to = step(y, by)
         net.send("y_2", ga2.at[lax.rem(to, 2), :, :, lax.div(to, 2)], ra2.at[by - 1], y=by)
     net.wait("y_1")
     gb2[...] = four(grad[yl, :, :, :, yh, :, right], gb1).astype(BF16)
-    for by in (1, 3, 2):
+    for by in (2, 1, 3):
         net.send("x_2", gb2.at[:, :, step(x, by)], rb2.at[by - 1], x=by)
     net.wait("y_2")
     fin[:, :, :, left] = four(ga2[yl, :, :, yh], ra2)
     net.wait("x_2")
     fin[:, :, :, right] = four(gb2[:, :, x], rb2)
 
-    for by, core in ((0, 1), (1, 0), (3, 0), (1, 1), (3, 1), (2, 0), (2, 1)):
+    for by, core in ((2, 1), (2, 0), (1, 1), (3, 1), (1, 0), (3, 0), (0, 1)):
         ref = fin.at[step(z, by), lax.rem(c + core, 2)]
         net.send("rows", ref, o_r.at[z, c], z=by, c=core)
     o_r[z, c] = fin[z, c]

time: 131 us -> 130 us (level)
  no operation moved by 1% of the time
where the time goes in v5:
time: 130 us
  Pallas kernels  128 us (98%)
  local copies, waits for them, and re-layouts  1.57 us (1%)
    pallas_call x1, Pallas kernels, per_device(): pl.pallas_call(kernel, out_shape=jax.ShapeDtypeStruct((16, 2048), F32), i...  128 us

profile of v5, /device:TPU:1, one launch (start us, length us, event | category | flops | bytes accessed | tf_op | source)
XLA Modules:
  0.0 129.8 jit_solution(6076657857155881673)
XLA Ops:
  0.0 128.2 %shard_map.82 = f32[16,2048]{1,0:T(8,128)} custom-call(bf16[4,320,1024]{2,1,0:T(8,128)(2,1)} %bitcast.3, bf16[1024,4096]{1,0:T(8,128)(2,1)} %w_in.1, bf16[160,4096]{1,0:T(8,128)(2,1)} %r_in.1, f32[1,4096]{1,0:T(1,128)} %bitcast.5, bf16[2,256,2048]{2,1,0:T(8,128)(2,1)} %bitcast.4, bf16[160,2048]{1,0:T(8,128)(2,1)} %s_in.1, bf16[160,2048]{1,0:T(8,128)(2,1)} %sr_in.1, ...), custom_call_target="tpu_custom_call" | custom-call | flops 16000000000 | bytes 16000000 | tf_op jit(solution)/shard_map/pallas_call | solution.py:536
  128.2 1.6 %copy.10 = f32[16,2048]{1,0:T(8,128)} copy(f32[16,2048]{1,0:T(8,128)} %shard_map.82) | data formatting | bytes 262144
